TPU v7x, 32 devices: a whole 2x2x4 slice. The times are simulated.
32 devices in a mesh: list: 8 (over z, x), help: 4 (over y, core).
Axes of the slice: x: 2, y: 2, z: 4, core: 2. Of those that a mesh axis runs over, the one named last changes fastest.
Arguments:
- members: bfloat16 [131072, 768], P(('list', 'help')), may hold values from -6 to 6
- owner: int32 [131072, 1], P(('list', 'help')), may hold values from 0 to 15; in each aligned block of 4096 rows (0 to 4095, 4096 to 8191, ...) at most 512 rows name the same one
- seed_label: int32 [131072], P(('list', 'help')), may hold values from 0 to 7
Outputs:
- assignments: float32 [8, 131072], P(None, ('list', 'help'))
- centroids: float32 [16, 8, 768], P('list')
Inputs may be any that keep to these rules, and one draw needn't show every extreme that they name: `owner`: in each device's block of 4096 members no list is named by more than 512 of them, a bound that some block reaches; every list has members.
All inputs are finite; a program needn't handle non-finite values.
Results may differ from a plain program's by a relative error of at most 0.012.
The roundings to bfloat16 on the way count: a program that leaves them out, or rounds other values in their place, can miss the bound.
Values may be sent and summed in bfloat16 or wider, within the bound.
A program may use at most 128 MiB of HBM per device.

v0:
```python
import jax
import jax.numpy as jnp
from jax import lax
from jax.sharding import PartitionSpec as P

K = 8
ITERS = 3
LIST_DEV = 2


smoothing_heat_factor = 2.0


def local(members, owner, seed_label):
    row_count, width = members.shape
    n_list = lax.axis_size("list")
    lists_all = n_list * LIST_DEV
    owner_ids = owner[:, 0]
    list_iota = jnp.arange(lists_all, dtype=jnp.int32)
    group_iota = jnp.arange(K, dtype=jnp.int32)
    capacity = max(2, (2 * row_count + lists_all - 1) // lists_all)
    per_index = LIST_DEV * capacity
    list_hot_int = (owner_ids[:, None] == list_iota[None, :]).astype(jnp.int32)
    rank_in = jnp.sum(jnp.cumsum(list_hot_int, axis=0) * list_hot_int, axis=1) - 1
    slot_pos = owner_ids * capacity + rank_in
    outgoing = jnp.zeros((lists_all * capacity, width), jnp.bfloat16).at[slot_pos].set(members)
    tags = (
        jnp.zeros((lists_all * capacity,), jnp.bfloat16)
        .at[slot_pos]
        .set((seed_label + 1).astype(jnp.bfloat16))
    )
    shipped = outgoing.reshape(n_list, per_index, width)
    shipped_tags = tags.reshape(n_list, per_index)
    arrived, received_labels_list = (
        lax.all_to_all(shipped, "list", split_axis=0, concat_axis=0, tiled=True),
        lax.all_to_all(shipped_tags, "list", split_axis=0, concat_axis=0, tiled=True),
    )
    arrived = arrived.reshape(n_list, LIST_DEV, capacity, width)
    tag_vals = received_labels_list.astype(jnp.float32).reshape(n_list, LIST_DEV, capacity)
    present = (tag_vals > 0.5).astype(jnp.float32)
    labels = tag_vals - 1.0

    def group_update(weights_bf):
        sums = jnp.einsum("sqck,sqcd->qkd", weights_bf, arrived, preferred_element_type=jnp.float32)
        totals = jnp.sum(weights_bf.astype(jnp.float32), axis=(0, 2))
        sums, totals = lax.psum((sums, totals), "help")
        return sums / (totals + 1.0)[:, :, None]

    def holder_mapping(centers):
        separation_measures = jnp.einsum(
            "sqcd,qkd->sqck",
            arrived,
            centers.astype(jnp.bfloat16),
            preferred_element_type=jnp.float32,
        )
        centroid_magnitude_power = jnp.sum(centers * centers, axis=-1)[None, :, None, :]
        membership_raw_preference = (
            2.0 * separation_measures - centroid_magnitude_power
        ) / smoothing_heat_factor
        return jax.nn.softmax(membership_raw_preference, axis=-1)

    init_weights = (labels[..., None] == group_iota.astype(jnp.float32)).astype(jnp.bfloat16)
    centers = group_update(init_weights)
    for turn in range(ITERS):
        weights = (holder_mapping(centers) * present[..., None]).astype(jnp.bfloat16)
        centers = group_update(weights)
    final = holder_mapping(centers)
    going_back = jnp.transpose(final, (3, 0, 1, 2)).reshape(K, n_list, per_index)
    returned = lax.all_to_all(going_back, "list", split_axis=1, concat_axis=1, tiled=True)
    assignments = returned.reshape(K, n_list * per_index)[:, slot_pos]
    return (assignments, centers)


def solution(mesh):
    placed = (P(("list", "help"), None), P(("list", "help"), None), P(("list", "help")))
    return jax.shard_map(
        local,
        mesh=mesh,
        in_specs=placed,
        out_specs=(P(None, ("list", "help")), P("list", None, None)),
        check_vma=False,
    )
```

profile of v0, /device:TPU:0, one launch (start us, length us, event | category | flops | bytes accessed | tf_op | source)
XLA Modules:
  0.0 474.6 jit_solution(1660549068840220694)
XLA Ops:
  0.6 0.7 fusion.88
  1.4 4.6 reduce-window.6
  6.0 0.5 slice_reduce_fusion
  6.5 0.2 reduce-window.9
  6.6 0.1 broadcast_add_fusion
  6.8 0.9 fusion.80
  7.7 0.7 compare_select_fusion
  8.5 0.7 add_convert_fusion
  9.2 28.6 %scatter_custom_fusion = bf16[8192]{0:T(1024)(128)(2,1)S(1)} fusion(s32[4096]{0:T(1024)S(1)} %bitcast.113, bf16[4096]{0:T(1024)(128)(2,1)S(1)} %add_convert_fusion, bf16[]{:T(256)} %constant.12.clone.1), kind=kCustom, calls=%fused_computation.100 | custom fusion | bytes 16386 | tf_op jit(solution)/shard_map/scatter | solution.py:30
  37.8 0.5 broadcast.155
  38.3 0.7 reduce.6
  39.0 0.6 reshape.131
  39.7 7.3 %all-to-all-start = ((bf16[8,2,512]{2,1,0:T(2,128)(2,1)}), bf16[8,2,512]{2,1,0:T(2,128)(2,1)S(1)}, u32[]{:S(2)}, u32[]{:S(2)}) async-start(bf16[8,2,512]{2,1,0:T(2,128)(2,1)} %reshape.131), calls=%async_computation | async-start | bytes 32768 | tf_op jit(solution)/shard_map/all_to_all | solution.py:36
  46.9 26.0 %scatter_custom_fusion.1 = bf16[8192,768]{1,0:T(8,128)(2,1)} fusion(s32[4096]{0:T(1024)S(1)} %bitcast.114, bf16[4096,768]{1,0:T(8,128)(2,1)} %param.3, bf16[]{:T(256)} %constant.12.clone.1), kind=kCustom, calls=%fused_computation.6 | custom fusion | bytes 12583424 | tf_op jit(solution)/shard_map/scatter | solution.py:26
  72.9 0.0 all-to-all-done
  72.9 6.0 %all-to-all-start.1 = ((bf16[8,1024,768]{2,1,0:T(8,128)(2,1)}), bf16[8,1024,768]{2,1,0:T(8,128)(2,1)}, u32[]{:S(2)}, u32[]{:S(2)}) async-start(bf16[8,1024,768]{2,1,0:T(8,128)(2,1)} %bitcast.102), calls=%async_computation.1 | async-start | bytes 25165824 | tf_op jit(solution)/shard_map/all_to_all | solution.py:35
  79.0 0.2 fusion.91
  79.1 0.2 convert_reduce_fusion.3
  79.3 272.1 %all-to-all-done.1 = bf16[8,1024,768]{2,1,0:T(8,128)(2,1)} async-done(((bf16[8,1024,768]{2,1,0:T(8,128)(2,1)}), bf16[8,1024,768]{2,1,0:T(8,128)(2,1)}, u32[]{:S(2)}, u32[]{:S(2)}) %all-to-all-start.1) | async-done | bytes 12582944 | tf_op jit(solution)/shard_map/all_to_all | solution.py:35
  351.4 5.6 %fusion.66 = f32[2,8,768]{2,1,0:T(8,128)S(1)} fusion(bf16[8,2,512,768]{3,2,1,0:T(8,128)(2,1)} %bitcast.6, f32[8,2,512]{2,0,1:T(8,128)S(1)} %bitcast.105, f32[8]{0:T(128)S(1)} %iota_convert_fusion), kind=kOutput, calls=%fused_computation.43 | convolution fusion | flops 100728832 | bytes 12664864 | tf_op jit(solution)/shard_map/sqck,sqcd->qkd/dot_general | solution.py:44
  357.0 10.7 %all-reduce.3 = (f32[2,8,768]{2,1,0:T(8,128)S(1)}, f32[2,8]{1,0:T(2,128)S(1)}) all-reduce(f32[2,8,768]{2,1,0:T(8,128)S(1)} %fusion.66, f32[2,8]{1,0:T(2,128)S(1)} %convert_reduce_fusion.3), channel_id=1, replica_groups=mesh['list'=8,'help'=4] {'help'}, use_global_device_ids=true, to_apply=%region_5.6 | all-reduce | flops 12304 | bytes 98432 | tf_op jit(solution)/shard_map/psum | solution.py:46
  367.6 0.2 multiply_reduce_fusion.3
  367.8 6.4 %fusion.102 = (f32[8,2,512]{2,0,1:T(8,128)S(1)}, f32[8,2,512,8]{2,3,0,1:T(8,128)S(1)}) fusion(bf16[8,2,512,768]{3,2,1,0:T(8,128)(2,1)} %bitcast.6, f32[2,8]{1,0:T(2,128)S(1)} %multiply_reduce_fusion.3, f32[2,8,768]{2,1,0:T(8,128)S(1)} %get-tuple-element.16, f32[2,8]{1,0:T(2,128)S(1)} %broadcast_add_fusion.5), kind=kOutput, calls=%fused_computation.107 | convolution fusion | flops 101015560 | bytes 12927104 | tf_op jit(solution)/shard_map/sub | solution.py:60
  374.2 0.1 convert_reduce_fusion.2
  374.4 5.5 %fusion.69 = f32[2,8,768]{2,1,0:T(8,128)S(1)} fusion(bf16[8,2,512,8]{2,3,0,1:T(8,128)(2,1)S(1)} %get-tuple-element.25, bf16[8,2,512,768]{3,2,1,0:T(8,128)(2,1)} %bitcast.6), kind=kOutput, calls=%fused_computation.44 | convolution fusion | flops 100663296 | bytes 12763136 | tf_op jit(solution)/shard_map/sqck,sqcd->qkd/dot_general | solution.py:44
  379.9 11.4 %all-reduce.2 = (f32[2,8,768]{2,1,0:T(8,128)S(1)}, f32[2,8]{1,0:T(2,128)S(1)}) all-reduce(f32[2,8,768]{2,1,0:T(8,128)S(1)} %fusion.69, f32[2,8]{1,0:T(2,128)S(1)} %get-tuple-element.24), channel_id=1, replica_groups=mesh['list'=8,'help'=4] {'help'}, use_global_device_ids=true, to_apply=%region_11.12 | all-reduce | flops 12304 | bytes 98432 | tf_op jit(solution)/shard_map/psum | solution.py:46
  391.3 0.2 multiply_reduce_fusion.2
  391.5 6.4 %fusion.103 = (f32[8,2,512]{2,0,1:T(8,128)S(1)}, f32[8,2,512,8]{2,3,0,1:T(8,128)S(1)}) fusion(bf16[8,2,512,768]{3,2,1,0:T(8,128)(2,1)} %bitcast.6, f32[2,8]{1,0:T(2,128)S(1)} %multiply_reduce_fusion.2, f32[2,8,768]{2,1,0:T(8,128)S(1)} %get-tuple-element.14, f32[2,8]{1,0:T(2,128)S(1)} %broadcast_add_fusion.4), kind=kOutput, calls=%fused_computation.108 | convolution fusion | flops 101015560 | bytes 12927104 | tf_op jit(solution)/shard_map/sub | solution.py:60
  397.9 0.1 convert_reduce_fusion.1
  398.1 5.5 %fusion.72 = f32[2,8,768]{2,1,0:T(8,128)S(1)} fusion(bf16[8,2,512,8]{2,3,0,1:T(8,128)(2,1)S(1)} %get-tuple-element.23, bf16[8,2,512,768]{3,2,1,0:T(8,128)(2,1)} %bitcast.6), kind=kOutput, calls=%fused_computation.45 | convolution fusion | flops 100663296 | bytes 12763136 | tf_op jit(solution)/shard_map/sqck,sqcd->qkd/dot_general | solution.py:44
  403.6 11.2 %all-reduce.1 = (f32[2,8,768]{2,1,0:T(8,128)S(1)}, f32[2,8]{1,0:T(2,128)S(1)}) all-reduce(f32[2,8,768]{2,1,0:T(8,128)S(1)} %fusion.72, f32[2,8]{1,0:T(2,128)S(1)} %get-tuple-element.22), channel_id=1, replica_groups=mesh['list'=8,'help'=4] {'help'}, use_global_device_ids=true, to_apply=%region_17.18 | all-reduce | flops 12304 | bytes 98432 | tf_op jit(solution)/shard_map/psum | solution.py:46
  414.8 0.2 multiply_reduce_fusion.1
  414.9 6.4 %fusion.104 = (f32[8,2,512]{2,0,1:T(8,128)S(1)}, f32[8,2,512,8]{2,3,0,1:T(8,128)S(1)}) fusion(bf16[8,2,512,768]{3,2,1,0:T(8,128)(2,1)} %bitcast.6, f32[2,8]{1,0:T(2,128)S(1)} %multiply_reduce_fusion.1, f32[2,8,768]{2,1,0:T(8,128)S(1)} %get-tuple-element.12, f32[2,8]{1,0:T(2,128)S(1)} %broadcast_add_fusion.3), kind=kOutput, calls=%fused_computation.109 | convolution fusion | flops 101015560 | bytes 12927104 | tf_op jit(solution)/shard_map/sub | solution.py:60
  421.4 0.1 convert_reduce_fusion
  421.5 5.5 %fusion.75 = f32[2,8,768]{2,1,0:T(8,128)S(1)} fusion(bf16[8,2,512,8]{2,3,0,1:T(8,128)(2,1)S(1)} %get-tuple-element.21, bf16[8,2,512,768]{3,2,1,0:T(8,128)(2,1)} %bitcast.6), kind=kOutput, calls=%fused_computation.46 | convolution fusion | flops 100663296 | bytes 12763136 | tf_op jit(solution)/shard_map/sqck,sqcd->qkd/dot_general | solution.py:44
  427.0 10.8 %all-reduce = (f32[2,8,768]{2,1,0:T(8,128)S(1)}, f32[2,8]{1,0:T(2,128)S(1)}) all-reduce(f32[2,8,768]{2,1,0:T(8,128)S(1)} %fusion.75, f32[2,8]{1,0:T(2,128)S(1)} %get-tuple-element.20), channel_id=1, replica_groups=mesh['list'=8,'help'=4] {'help'}, use_global_device_ids=true, to_apply=%region_23.24 | all-reduce | flops 12304 | bytes 98432 | tf_op jit(solution)/shard_map/psum | solution.py:46
  437.8 0.2 multiply_reduce_fusion
  438.0 0.0 copy-start
  438.0 6.4 %bitcast_reduce_fusion = (f32[8,2,512]{2,0,1:T(8,128)S(1)}, f32[2,8,8,512]{3,1,2,0:T(8,128)S(1)}) fusion(f32[2,8]{1,0:T(2,128)S(1)} %get-tuple-element.18, bf16[8,2,512,768]{3,2,1,0:T(8,128)(2,1)} %bitcast.6, f32[2,8,768]{2,1,0:T(8,128)S(1)} %get-tuple-element.19), kind=kOutput, calls=%fused_computation.54 | convolution fusion | flops 100929536 | bytes 12927040 | tf_op jit(solution)/shard_map/sqcd,qkd->sqck/dot_general | solution.py:50
  444.4 0.2 fusion.82
  444.6 0.1 fusion.87
  444.7 0.7 copy.44
  445.4 3.6 all-to-all-start.2
  449.1 8.8 %all-to-all-done.2 = f32[8,8,1024]{2,0,1:T(8,128)S(1)} async-done(((f32[8,8,1024]{2,0,1:T(8,128)}), f32[8,8,1024]{2,0,1:T(8,128)S(1)}, u32[]{:S(2)}, u32[]{:S(2)}) %all-to-all-start.2) | async-done | bytes 262176 | tf_op jit(solution)/shard_map/all_to_all | solution.py:69
  457.9 2.6 copy.32
  460.4 13.0 %gather_fusion = f32[4096,8]{1,0:T(8,128)S(1)} fusion(f32[8,8192]{0,1:T(8,128)} %bitcast.103, s32[4096]{0:T(1024)S(1)} %broadcast_clamp_fusion), kind=kCustom, calls=%fused_computation | custom fusion | bytes 278528 | tf_op jit(solution)/shard_map/gather | solution.py:70
  473.4 1.2 copy.33
  474.6 0.0 copy-done
  (9 shorter events, 0.1 us)
Async XLA Ops:
  39.7 33.3 %all-to-all-start = ((bf16[8,2,512]{2,1,0:T(2,128)(2,1)}), bf16[8,2,512]{2,1,0:T(2,128)(2,1)S(1)}, u32[]{:S(2)}, u32[]{:S(2)}) async-start(bf16[8,2,512]{2,1,0:T(2,128)(2,1)} %reshape.131), calls=%async_computation | async-start | bytes 32768 | tf_op jit(solution)/shard_map/all_to_all | solution.py:36
  72.9 278.5 %all-to-all-start.1 = ((bf16[8,1024,768]{2,1,0:T(8,128)(2,1)}), bf16[8,1024,768]{2,1,0:T(8,128)(2,1)}, u32[]{:S(2)}, u32[]{:S(2)}) async-start(bf16[8,1024,768]{2,1,0:T(8,128)(2,1)} %bitcast.102), calls=%async_computation.1 | async-start | bytes 25165824 | tf_op jit(solution)/shard_map/all_to_all | solution.py:35
  438.0 36.6 %copy-start = (f32[2,8,768]{2,1,0:T(8,128)}, f32[2,8,768]{2,1,0:T(8,128)S(1)}, u32[]{:S(2)}) copy-start(f32[2,8,768]{2,1,0:T(8,128)S(1)} %get-tuple-element.19) | copy-start | bytes 147460
  445.4 12.4 %all-to-all-start.2 = ((f32[8,8,1024]{2,0,1:T(8,128)}), f32[8,8,1024]{2,0,1:T(8,128)S(1)}, u32[]{:S(2)}, u32[]{:S(2)}) async-start(f32[8,8,1024]{2,0,1:T(8,128)} %bitcast.38), calls=%async_computation.2 | async-start | bytes 524288 | tf_op jit(solution)/shard_map/all_to_all | solution.py:69
where the time goes:
time: 475 us
  waiting for transfers between devices  281 us (59%)
  local copies, waits for them, and re-layouts  73.7 us (16%)
  matrix products  47.7 us (10%)
  blocking collectives  44 us (9%)
  starting transfers between devices  16.9 us (4%)
  other arithmetic  10.6 us (2%)
    all_to_all x1, waiting for transfers between devices, local(): lax.all_to_all(shipped, 'list', split_axis=0, concat_axis=0, tiled=True)  272 us
    psum x4, blocking collectives, group_update(): sums, totals = lax.psum((sums, totals), 'help')  44 us
    scatter x1, local copies, waits for them, and re-layouts, local(): tags = jnp.zeros((lists_all * capacity,), jnp.bfloat16).at[slot_pos].set(...  28.6 us
    scatter x1, local copies, waits for them, and re-layouts, local(): jnp.zeros((lists_all * capacity, width), jnp.bfloat16).at[slot_pos]  26 us
    dot_general x4, matrix products, group_update(): jnp.einsum('sqck,sqcd->qkd', weights_bf, arrived, preferred_element_type=...  22.1 us
    sub x3, matrix products, holder_mapping(): return jax.nn.softmax(membership_raw_preference, axis=-1)  19.2 us
    gather x1, local copies, waits for them, and re-layouts, local(): assignments = returned.reshape(K, n_list * per_index)[:, slot_pos]  13 us
  transfers between devices with their start and end apart: 3, of which 2 were waited for; matrix products, arithmetic and copies ran while one was open for 6% of the time, Pallas kernels for 0%

commit v1 on v0

v1 whole, which is shorter than its diff:
```python
import jax
import jax.numpy as jnp
from jax import lax
from jax.sharding import PartitionSpec as P

K = 8
ITERS = 3
LIST_DEV = 2
HEAT = 2.0


def local(members, owner, seed_label):
    rows, width = members.shape
    lists = lax.axis_size("list") * LIST_DEV
    own = owner[:, 0]
    hot = own[None, :] == jnp.arange(lists, dtype=jnp.int32)[:, None]
    seeds = seed_label[None, :] == jnp.arange(K, dtype=jnp.int32)[:, None]

    def update(weights):
        spread = jnp.where(hot[:, None, :], weights[None], 0).astype(jnp.bfloat16)
        spread = spread.reshape(lists * K, rows)
        sums = jnp.dot(spread, members, preferred_element_type=jnp.float32)
        totals = jnp.sum(spread.astype(jnp.float32), axis=1, keepdims=True)
        both = jnp.concatenate([sums, jnp.broadcast_to(totals, (lists * K, 128))], axis=1)
        both = lax.psum(both, ("list", "help"))
        return both[:, :width] / (both[:, width : width + 1] + 1.0)

    def assign(centers):
        inner = lax.dot_general(
            centers.astype(jnp.bfloat16),
            members,
            (((1,), (1,)), ((), ())),
            preferred_element_type=jnp.float32,
        )
        power = jnp.sum(centers * centers, axis=1, keepdims=True)
        logits = (2.0 * inner - power) / HEAT
        logits = jnp.sum(jnp.where(hot[:, None, :], logits.reshape(lists, K, rows), 0.0), axis=0)
        return jax.nn.softmax(logits, axis=0)

    centers = update(jnp.where(seeds, 1.0, 0.0))
    for _ in range(ITERS):
        centers = update(assign(centers))
    out = assign(centers)
    mine = lax.axis_index("list") * LIST_DEV * K
    own_centers = lax.dynamic_slice_in_dim(centers, mine, LIST_DEV * K, 0)
    return out, own_centers.reshape(LIST_DEV, K, width)


def solution(mesh):
    placed = (P(("list", "help"), None), P(("list", "help"), None), P(("list", "help")))
    return jax.shard_map(
        local,
        mesh=mesh,
        in_specs=placed,
        out_specs=(P(None, ("list", "help")), P("list", None, None)),
        check_vma=False,
    )
```

time: 475 us -> 578 us (1.22)
  waiting for transfers between devices: 281 us -> 509 us
  local copies, waits for them, and re-layouts: 73.7 us -> 1.26 us
  blocking collectives: 44 us -> 0 us
  starting transfers between devices: 16.9 us -> 0.34 us
  between operations: 0.82 us -> 13.9 us
  matrix products: 47.7 us -> 35.7 us
    psum x0 -> x4, waiting for transfers between devices: none -> 509 us  [update(): both = lax.psum(both, ('list', 'help'))]
    all_to_all x3 -> x0, waiting for transfers between devices: 281 us -> none  [the longest x1 272 us: local(): lax.all_to_all(shipped, 'list', split_axis=0, concat_axis=0, tiled=True)]
    scatter x2 -> x0, local copies, waits for them, and re-layouts: 54.6 us -> none  [the longest x1 28.6 us: local(): tags = jnp.zeros((lists_all * capacity,), jnp.bfloat16).at[slot_pos].set(...]
    psum x4 -> x0, blocking collectives: 44 us -> none  [group_update(): sums, totals = lax.psum((sums, totals), 'help')]
    sub x3 -> x0, matrix products: 19.2 us -> none  [holder_mapping(): return jax.nn.softmax(membership_raw_preference, axis=-1)]
    all_to_all x3 -> x0, starting transfers between devices: 16.9 us -> none  [the longest x1 7.25 us: local(): lax.all_to_all(shipped_tags, 'list', split_axis=0, concat_axis=0, tiled=T...]
    gather x1 -> x0, local copies, waits for them, and re-layouts: 13 us -> none  [local(): assignments = returned.reshape(K, n_list * per_index)[:, slot_pos]]
    dot_general x5 -> x8, matrix products: 28.5 us -> 35.7 us  [the longest x4 20.5 us: assign(): lax.dot_general(centers.astype(jnp.bfloat16), members, (((1,), (1,)), (()...]
  transfers between devices with their start and end apart: 3 -> 4, of which waited for: 2 -> 4; matrix products, arithmetic and copies ran while one was open for 6% -> 0% of each run, Pallas kernels for 0% -> 0%
where the time goes in v1:
time: 578 us; the launch traced here: 577 us
  waiting for transfers between devices  509 us (88%)
  matrix products  35.7 us (6%)
  other arithmetic  16.2 us (3%)
  between operations  13.9 us (2%)
    psum x4, waiting for transfers between devices, update(): both = lax.psum(both, ('list', 'help'))  509 us
    dot_general x4, matrix products, assign(): lax.dot_general(centers.astype(jnp.bfloat16), members, (((1,), (1,)), (()...  20.5 us
    dot_general x4, matrix products, update(): sums = jnp.dot(spread, members, preferred_element_type=jnp.float32)  15.2 us
  transfers between devices with their start and end apart: 4, of which 4 were waited for; matrix products, arithmetic and copies ran while one was open for 0% of the time, Pallas kernels for 0%

profile of v1, /device:TPU:0, one launch (start us, length us, event | category | flops | bytes accessed | tf_op | source)
XLA Modules:
  0.0 576.9 jit_solution(10206829504065557843)
XLA Ops:
  7.2 0.0 all-reduce.5.cloned.1.call-start
  7.2 0.8 iota_compare_fusion
  8.0 0.7 fusion.48
  8.7 0.4 convert_reduce_fusion.3
  9.1 3.8 fusion.30
  12.9 0.1 broadcast_in_dim.146
  13.0 0.1 broadcast_in_dim.147
  13.1 0.8 pad_maximum_fusion
  13.9 0.0 all-reduce.5.cloned.1.call-update
  13.9 0.0 all-reduce.7.cloned.1.call-start
  14.0 128.7 %all-reduce.5.cloned.1.call-done = f32[128,896]{1,0:T(8,128)} async-done(((f32[128,896]{1,0:T(8,128)}), f32[128,896]{1,0:T(8,128)}) %all-reduce.5.cloned.1.call-update) | async-done | bytes 458768 | tf_op jit(solution)/shard_map/psum | solution.py:25
  142.7 0.9 fusion.60
  143.7 1.2 multiply_reduce_fusion.3
  144.9 5.2 fusion.23
  150.1 0.1 fusion.50
  150.2 3.8 fusion.28
  154.0 0.4 convert_reduce_fusion.2
  154.4 0.1 broadcast_in_dim.149
  154.5 0.1 broadcast_in_dim.150
  154.6 0.8 pad_maximum_fusion.1
  155.4 0.0 all-reduce.7.cloned.1.call-update
  155.4 0.0 all-reduce.9.cloned.1.call-start
  155.5 126.9 %all-reduce.7.cloned.1.call-done = f32[128,896]{1,0:T(8,128)} async-done(((f32[128,896]{1,0:T(8,128)}), f32[128,896]{1,0:T(8,128)}) %all-reduce.7.cloned.1.call-update) | async-done | bytes 458768 | tf_op jit(solution)/shard_map/psum | solution.py:25
  282.4 0.9 fusion.59
  283.3 1.2 multiply_reduce_fusion.2
  284.5 5.2 fusion.22
  289.8 0.1 fusion.52
  289.9 3.8 fusion.26
  293.7 0.4 convert_reduce_fusion.1
  294.1 0.1 broadcast_in_dim.152
  294.2 0.1 broadcast_in_dim.153
  294.2 0.8 pad_maximum_fusion.2
  295.1 0.0 all-reduce.9.cloned.1.call-update
  295.1 0.2 all-reduce.11.cloned.1.call-start
  295.3 126.8 %all-reduce.9.cloned.1.call-done = f32[128,896]{1,0:T(8,128)} async-done(((f32[128,896]{1,0:T(8,128)}), f32[128,896]{1,0:T(8,128)}) %all-reduce.9.cloned.1.call-update) | async-done | bytes 458768 | tf_op jit(solution)/shard_map/psum | solution.py:25
  422.1 0.9 fusion.58
  423.0 1.2 multiply_reduce_fusion.1
  424.2 5.2 fusion.21
  429.4 0.1 fusion.54
  429.6 3.8 fusion.24
  433.4 0.4 convert_reduce_fusion
  433.8 0.1 broadcast_in_dim.155
  433.9 0.1 broadcast_in_dim.156
  433.9 0.8 pad_maximum_fusion.3
  434.8 0.0 all-reduce.11.cloned.1.call-update
  434.8 127.0 %all-reduce.11.cloned.1.call-done = f32[128,896]{1,0:T(8,128)} async-done(((f32[128,896]{1,0:T(8,128)}), f32[128,896]{1,0:T(8,128)}) %all-reduce.11.cloned.1.call-update) | async-done | bytes 458768 | tf_op jit(solution)/shard_map/psum | solution.py:25
  561.8 0.9 fusion.57
  562.7 1.2 multiply_reduce_fusion
  563.9 5.0 fusion.20
  569.0 0.1 fusion.56
  569.0 0.7 fusion.55
  569.7 0.6 dynamic-slice_bitcast_fusion
  (7 shorter events, 0.3 us)
Async XLA Ops:
  7.2 135.6 %all-reduce.5.cloned.1.call-start = ((), (), s32[]{:S(2)}) async-start(), calls=%async_computation | async-start | bytes 917504 | tf_op jit(solution)/shard_map/psum | solution.py:25
  13.9 268.5 %all-reduce.7.cloned.1.call-start = ((), (), s32[]{:S(2)}) async-start(), calls=%async_computation.1 | async-start | bytes 917504 | tf_op jit(solution)/shard_map/psum | solution.py:25
  155.4 266.6 %all-reduce.9.cloned.1.call-start = ((), (), s32[]{:S(2)}) async-start(), calls=%async_computation.2 | async-start | bytes 917504 | tf_op jit(solution)/shard_map/psum | solution.py:25
  295.1 266.7 %all-reduce.11.cloned.1.call-start = ((), (), s32[]{:S(2)}) async-start(), calls=%async_computation.3 | async-start | bytes 917504 | tf_op jit(solution)/shard_map/psum | solution.py:25
Sparse Core Ops, SparseCore 0:
  14.0 128.6 all-reduce.4
  155.6 126.7 all-reduce.6
  295.2 126.8 all-reduce.8
  434.9 126.8 all-reduce.10

commit v2 on v1

v2 whole, which is shorter than its diff:
```python
import functools
import jax
import jax.numpy as jnp
from jax import lax
from jax.experimental import pallas as pl
from jax.experimental.pallas import tpu as pltpu
from jax.sharding import PartitionSpec as P

K = 8
ITERS = 3
LIST_DEV = 2
TILE = 1024
LANES = 128
MESH = pl.DeviceIdType.MESH


def kernel(
    n_list, n_help, members, own, seed, out, cent,
    acc, theirs, part, gathered, packs, table, power, mine, wide_table,
    sib_send, sib_recv, rs_send, rs_recv, ag_send, ag_recv, fin_send, fin_recv,
):
    rows, width = members.shape
    half = width // 2
    lists = n_list * LIST_DEV
    per_list = n_help // 2
    units = n_list * per_list
    i_list = lax.axis_index("list")
    i_help = lax.axis_index("help")
    core = lax.rem(i_help, 2)
    unit = i_list * per_list + i_help // 2

    def device_of(u, c):
        return (u // per_list, lax.rem(u, per_list) * 2 + c)

    sibling = (i_list, i_help + 1 - 2 * core)

    barrier = pltpu.get_barrier_semaphore()

    @pl.loop(1, units)
    def _(d):
        pl.semaphore_signal(
            barrier, inc=1, device_id=device_of(lax.rem(unit + d, units), core), device_id_type=MESH
        )

    for d in range(1, n_help):
        to = lax.rem(i_help + d, n_help)

        @pl.when(lax.rem(to, 2) != core)
        def _():
            pl.semaphore_signal(barrier, inc=1, device_id=(i_list, to), device_id_type=MESH)

    pl.semaphore_wait(barrier, units - 1 + per_list)

    def rs_copy(d, to, slot):
        return pltpu.make_async_remote_copy(
            src_ref=part.at[to], dst_ref=gathered.at[slot],
            send_sem=rs_send.at[d], recv_sem=rs_recv.at[d],
            device_id=device_of(to, core), device_id_type=MESH,
        )

    def ag_copy(d, to, slot):
        return pltpu.make_async_remote_copy(
            src_ref=packs.at[core, unit], dst_ref=packs.at[core, slot],
            send_sem=ag_send.at[d], recv_sem=ag_recv.at[d],
            device_id=device_of(to, core), device_id_type=MESH,
        )

    def assign(t):
        cols = pl.ds(pl.multiple_of(t * TILE, TILE), TILE)
        inner = lax.dot_general(
            table[...], members[cols, :], (((1,), (1,)), ((), ())),
            preferred_element_type=jnp.float32,
        )
        owner = jnp.broadcast_to(own[:, cols], (K, TILE))
        logit = jnp.zeros((K, TILE), jnp.float32)
        for l in range(lists):
            row = slice(l * K, (l + 1) * K)
            logit = jnp.where(owner == l, inner[row] - power[row, 0:1], logit)
        e = jnp.exp(logit - jnp.max(logit, axis=0, keepdims=True))
        return e / jnp.sum(e, axis=0, keepdims=True)

    def seeded(t):
        cols = pl.ds(pl.multiple_of(t * TILE, TILE), TILE)
        label = jnp.broadcast_to(seed[:, cols], (K, TILE))
        return jnp.where(label == lax.broadcasted_iota(jnp.int32, (K, TILE), 0), 1.0, 0.0)

    def accumulate(weigh):
        for h in range(2):
            acc[h] = jnp.zeros(acc.shape[1:], jnp.float32)

        @pl.loop(0, rows // TILE)
        def _(t):
            cols = pl.ds(pl.multiple_of(t * TILE, TILE), TILE)
            weight = weigh(t).astype(jnp.bfloat16).astype(jnp.float32)
            owner = jnp.broadcast_to(own[:, cols], (K, TILE))
            spread = jnp.concatenate(
                [jnp.where(owner == l, weight, 0.0) for l in range(lists)], axis=0
            )
            sums = jnp.dot(
                spread.astype(jnp.bfloat16), members[cols, :], preferred_element_type=jnp.float32
            )
            total = spread[:, :LANES]
            for j in range(1, TILE // LANES):
                total = total + spread[:, j * LANES : (j + 1) * LANES]
            for h in range(2):
                acc[h, :, :half] += sums[:, h * half : (h + 1) * half]
                acc[h, :, half:] += total

    def exchange():
        swap = pltpu.make_async_remote_copy(
            src_ref=acc.at[1 - core], dst_ref=theirs,
            send_sem=sib_send.at[0], recv_sem=sib_recv.at[0],
            device_id=sibling, device_id_type=MESH,
        )
        swap.start()
        swap.wait()
        both = acc[core] + theirs[...]
        part[...] = both.reshape(part.shape)

        @pl.loop(1, units)
        def _(d):
            rs_copy(d, lax.rem(unit + d, units), unit).start()

        gathered[unit] = part[unit]

        @pl.loop(1, units)
        def _(d):
            rs_copy(d, lax.rem(unit + d, units), lax.rem(unit + units - d, units)).wait()

        block = gathered[0]
        for u in range(1, units):
            block = block + gathered[u]
        total = jnp.sum(block[:, half:], axis=1, keepdims=True)
        centers = block[:, :half] / (total + 1.0)
        mine[...] = centers
        norm = 0.5 * jnp.sum(centers * centers, axis=1, keepdims=True)
        hi = norm.astype(jnp.bfloat16).astype(jnp.float32)
        mid = (norm - hi).astype(jnp.bfloat16).astype(jnp.float32)
        lo = norm - hi - mid
        lane = lax.broadcasted_iota(jnp.int32, (K, LANES), 1)
        tail = jnp.where(lane == 0, hi, jnp.where(lane == 1, mid, jnp.where(lane == 2, lo, 0.0)))
        wide = jnp.concatenate([centers, tail], axis=1)
        side = wide.shape[1] // 2
        packs[core, unit] = jnp.concatenate(
            [wide[:, :side], wide[:, side:]], axis=0
        ).astype(jnp.bfloat16)

        @pl.loop(1, units)
        def _(d):
            ag_copy(d, lax.rem(unit + d, units), unit).start()

        @pl.loop(1, units)
        def _(d):
            ag_copy(d, lax.rem(unit + d, units), lax.rem(unit + units - d, units)).wait()

        forward = pltpu.make_async_remote_copy(
            src_ref=packs.at[core], dst_ref=packs.at[core],
            send_sem=sib_send.at[1], recv_sem=sib_recv.at[1],
            device_id=sibling, device_id_type=MESH,
        )
        forward.start()
        forward.wait_send()
        pltpu.make_async_remote_copy(
            src_ref=packs.at[core], dst_ref=packs.at[1 - core],
            send_sem=sib_send.at[1], recv_sem=sib_recv.at[1],
            device_id=sibling, device_id_type=MESH,
        ).wait_recv()

        for l in range(lists):
            whole, norms = [], 0.0
            for h in range(2):
                got = packs[h, l].astype(jnp.float32)
                got = jnp.concatenate([got[:K], got[K:]], axis=1)
                whole.append(got[:, :half])
                norms = norms + jnp.sum(got[:, half:], axis=1, keepdims=True)
            power[l * K : (l + 1) * K, :] = jnp.broadcast_to(norms, (K, LANES))
            wide_table[l] = jnp.concatenate(whole, axis=1)
        table[...] = wide_table[...].reshape(table.shape).astype(jnp.bfloat16)

    accumulate(seeded)
    exchange()

    @pl.loop(0, ITERS)
    def _(turn):
        accumulate(assign)
        exchange()

    def fin_copy(d, slot):
        return pltpu.make_async_remote_copy(
            src_ref=mine, dst_ref=cent.at[slot],
            send_sem=fin_send.at[d], recv_sem=fin_recv.at[d],
            device_id=(i_list, lax.rem(i_help + d, n_help)), device_id_type=MESH,
        )

    for d in range(1, n_help):
        fin_copy(d, i_help).start()
    cent[i_help] = mine[...]

    @pl.loop(0, rows // TILE)
    def _(t):
        cols = pl.ds(pl.multiple_of(t * TILE, TILE), TILE)
        out[:, cols] = assign(t)

    for d in range(1, n_help):
        fin_copy(d, lax.rem(i_help + n_help - d, n_help)).wait()


def local(members, owner, seed_label):
    rows, width = members.shape
    n_list, n_help = lax.axis_size("list"), lax.axis_size("help")
    lists = n_list * LIST_DEV
    units = n_list * n_help // 2
    half = width // 2
    packed = half + LANES
    vmem = pl.BlockSpec(memory_space=pltpu.VMEM)
    dma = pltpu.SemaphoreType.DMA
    out, cent = pl.pallas_call(
        functools.partial(kernel, n_list, n_help),
        out_shape=(
            jax.ShapeDtypeStruct((K, rows), jnp.float32),
            jax.ShapeDtypeStruct((n_help, K, half), jnp.float32),
        ),
        in_specs=[vmem] * 3,
        out_specs=(vmem, vmem),
        scratch_shapes=[
            pltpu.VMEM((2, lists * K, packed), jnp.float32),
            pltpu.VMEM((lists * K, packed), jnp.float32),
            pltpu.VMEM((units, K, packed), jnp.float32),
            pltpu.VMEM((units, K, packed), jnp.float32),
            pltpu.VMEM((2, units, 2 * K, packed // 2), jnp.bfloat16),
            pltpu.VMEM((lists * K, width), jnp.bfloat16),
            pltpu.VMEM((lists * K, LANES), jnp.float32),
            pltpu.VMEM((K, half), jnp.float32),
            pltpu.VMEM((lists, K, width), jnp.float32),
            dma((2,)),
            dma((2,)),
            dma((units,)),
            dma((units,)),
            dma((units,)),
            dma((units,)),
            dma((n_help,)),
            dma((n_help,)),
        ],
        compiler_params=pltpu.CompilerParams(
            collective_id=0, has_side_effects=True, vmem_limit_bytes=48 * 1024 * 1024
        ),
    )(members, owner.reshape(1, rows), seed_label.reshape(1, rows))
    cent = cent.reshape(n_help // 2, 2, K, half).transpose(0, 2, 1, 3)
    return out, cent.reshape(LIST_DEV, K, width)


def solution(mesh):
    placed = (P(("list", "help"), None), P(("list", "help"), None), P(("list", "help")))
    return jax.shard_map(
        local,
        mesh=mesh,
        in_specs=placed,
        out_specs=(P(None, ("list", "help")), P("list", None, None)),
        check_vma=False,
    )
```

time: 578 us -> 97.4 us (0.17)
  waiting for transfers between devices: 509 us -> 0 us
  Pallas kernels: 0 us -> 93.7 us
  matrix products: 35.7 us -> 0 us
  other arithmetic: 16.2 us -> 0 us
  between operations: 13.9 us -> 0.65 us
    psum x4 -> x0, waiting for transfers between devices: 509 us -> none  [update(): both = lax.psum(both, ('list', 'help'))]
    pallas_call x0 -> x1, Pallas kernels: none -> 93.7 us  [local(): pl.pallas_call(functools.partial(kernel, n_list, n_help), out_shape=(jax....]
    dot_general x8 -> x0, matrix products: 35.7 us -> none  [the longest x4 20.5 us: assign(): lax.dot_general(centers.astype(jnp.bfloat16), members, (((1,), (1,)), (()...]
    reduce_sum x12 -> x0, other arithmetic: 6.58 us -> none  [the longest x4 4.78 us: assign(): power = jnp.sum(centers * centers, axis=1, keepdims=True)]
  transfers between devices with their start and end apart: 4 -> 0, of which waited for: 4 -> 0; matrix products, arithmetic and copies ran while one was open for 0% -> 0% of each run, Pallas kernels for 0% -> 0%
where the time goes in v2:
time: 97.4 us; the launch traced here: 97.1 us
  Pallas kernels  93.7 us (96%)
  local copies, waits for them, and re-layouts  2.7 us (3%)
    pallas_call x1, Pallas kernels, local(): pl.pallas_call(functools.partial(kernel, n_list, n_help), out_shape=(jax....  93.7 us
    unnamed x6, local copies, waits for them, and re-layouts  2.7 us

profile of v2, /device:TPU:0, one launch (start us, length us, event | category | flops | bytes accessed | tf_op | source)
XLA Modules:
  0.0 97.1 jit_solution(2486671503681691576)
XLA Ops:
  0.6 0.0 copy-start
  0.6 0.7 copy-done
  1.3 0.0 copy-start.1
  1.4 0.7 copy-done.1
  2.1 93.7 %shard_map.50 = (f32[8,4096]{1,0:T(8,128)S(1)}, f32[4,8,384]{2,1,0:T(8,128)S(1)}) custom-call(bf16[4096,768]{1,0:T(8,128)(2,1)} %members.1, s32[1,4096]{1,0:T(1,128)S(1)} %bitcast.8, s32[1,4096]{1,0:T(1,128)S(1)} %bitcast.9), custom_call_target="tpu_custom_call" | custom-call | tf_op jit(solution)/shard_map/pallas_call | solution.py:217
  95.8 0.7 copy.7
  96.4 0.6 copy.8
Async XLA Ops:
  0.6 0.7 copy-start
  1.3 0.7 copy-start.1

commit v3 on v2

--- a/solution.py
+++ b/solution.py
@@ -15,9 +15,9 @@
 
 
 def kernel(
-    n_list, n_help, members, own, seed, out, cent,
-    acc, theirs, part, gathered, packs, table, power, mine, wide_table,
-    sib_send, sib_recv, rs_send, rs_recv, ag_send, ag_recv, fin_send, fin_recv,
+    n_list, n_help, source, own, seed, out, cent,
+    members, weights, count, acc, theirs, part, gathered, packs, table, power, mine, wide_table,
+    sib_send, sib_recv, rs_send, rs_recv, ag_send, ag_recv, fin_send, fin_recv, load_sem,
 ):
     rows, width = members.shape
     half = width // 2
@@ -29,17 +29,23 @@
     core = lax.rem(i_help, 2)
     unit = i_list * per_list + i_help // 2
 
+    def wrap(u):
+        return jnp.where(u >= units, u - units, u)
+
     def device_of(u, c):
         return (u // per_list, lax.rem(u, per_list) * 2 + c)
 
     sibling = (i_list, i_help + 1 - 2 * core)
+
+    load = pltpu.make_async_copy(source, members, load_sem)
+    load.start()
 
     barrier = pltpu.get_barrier_semaphore()
 
     @pl.loop(1, units)
     def _(d):
         pl.semaphore_signal(
-            barrier, inc=1, device_id=device_of(lax.rem(unit + d, units), core), device_id_type=MESH
+            barrier, inc=1, device_id=device_of(wrap(unit + d), core), device_id_type=MESH
         )
 
     for d in range(1, n_help):
@@ -49,21 +55,38 @@
         def _():
             pl.semaphore_signal(barrier, inc=1, device_id=(i_list, to), device_id_type=MESH)
 
-    pl.semaphore_wait(barrier, units - 1 + per_list)
-
-    def rs_copy(d, to, slot):
+    def arrive():
+        load.wait()
+        pl.semaphore_wait(barrier, units - 1 + per_list)
+
+    def swap_copy(q):
         return pltpu.make_async_remote_copy(
-            src_ref=part.at[to], dst_ref=gathered.at[slot],
-            send_sem=rs_send.at[d], recv_sem=rs_recv.at[d],
-            device_id=device_of(to, core), device_id_type=MESH,
-        )
-
-    def ag_copy(d, to, slot):
-        return pltpu.make_async_remote_copy(
-            src_ref=packs.at[core, unit], dst_ref=packs.at[core, slot],
-            send_sem=ag_send.at[d], recv_sem=ag_recv.at[d],
-            device_id=device_of(to, core), device_id_type=MESH,
-        )
+            src_ref=acc.at[q, 1 - core], dst_ref=theirs.at[q],
+            send_sem=sib_send.at[q], recv_sem=sib_recv.at[q],
+            device_id=sibling, device_id_type=MESH,
+        )
+
+    def scatter(q):
+        swap_copy(q).wait()
+        part[q] = (acc[q, core] + theirs[q]).reshape(part.shape[1:])
+
+        @pl.loop(1, units)
+        def _(d):
+            to = wrap(unit + d)
+            pltpu.make_async_remote_copy(
+                src_ref=part.at[q, to], dst_ref=gathered.at[q, unit],
+                send_sem=rs_send.at[q], recv_sem=rs_recv.at[q],
+                device_id=device_of(to, core), device_id_type=MESH,
+            ).start()
+
+        gathered[q, unit] = part[q, unit]
+
+    def scatter_wait(q):
+        pltpu.make_async_remote_copy(
+            src_ref=part.at[q, : units - 1], dst_ref=gathered.at[q, : units - 1],
+            send_sem=rs_send.at[q], recv_sem=rs_recv.at[q],
+            device_id=sibling, device_id_type=MESH,
+        ).wait()
 
     def assign(t):
         cols = pl.ds(pl.multiple_of(t * TILE, TILE), TILE)
@@ -84,9 +107,8 @@
         label = jnp.broadcast_to(seed[:, cols], (K, TILE))
         return jnp.where(label == lax.broadcasted_iota(jnp.int32, (K, TILE), 0), 1.0, 0.0)
 
-    def accumulate(weigh):
-        for h in range(2):
-            acc[h] = jnp.zeros(acc.shape[1:], jnp.float32)
+    def weigh_all(weigh):
+        count[...] = jnp.zeros_like(count)
 
         @pl.loop(0, rows // TILE)
         def _(t):
@@ -96,42 +118,42 @@
             spread = jnp.concatenate(
                 [jnp.where(owner == l, weight, 0.0) for l in range(lists)], axis=0
             )
-            sums = jnp.dot(
-                spread.astype(jnp.bfloat16), members[cols, :], preferred_element_type=jnp.float32
-            )
+            weights[:, cols] = spread.astype(jnp.bfloat16)
             total = spread[:, :LANES]
             for j in range(1, TILE // LANES):
                 total = total + spread[:, j * LANES : (j + 1) * LANES]
-            for h in range(2):
-                acc[h, :, :half] += sums[:, h * half : (h + 1) * half]
-                acc[h, :, half:] += total
+            count[...] += total
+
+    def sum_columns(columns):
+        return jnp.dot(weights[...], columns, preferred_element_type=jnp.float32)
 
     def exchange():
-        swap = pltpu.make_async_remote_copy(
-            src_ref=acc.at[1 - core], dst_ref=theirs,
-            send_sem=sib_send.at[0], recv_sem=sib_recv.at[0],
-            device_id=sibling, device_id_type=MESH,
-        )
-        swap.start()
-        swap.wait()
-        both = acc[core] + theirs[...]
-        part[...] = both.reshape(part.shape)
-
-        @pl.loop(1, units)
-        def _(d):
-            rs_copy(d, lax.rem(unit + d, units), unit).start()
-
-        gathered[unit] = part[unit]
-
-        @pl.loop(1, units)
-        def _(d):
-            rs_copy(d, lax.rem(unit + d, units), lax.rem(unit + units - d, units)).wait()
-
-        block = gathered[0]
+        ends = jnp.concatenate(
+            [members[:, :LANES], members[:, half : half + LANES]], axis=1
+        )
+        sums = sum_columns(ends)
+        for h in range(2):
+            acc[0, h, :, :LANES] = sums[:, h * LANES : (h + 1) * LANES]
+            acc[0, h, :, LANES:] = count[...]
+        swap_copy(0).start()
+
+        def rest(h):
+            start = pl.multiple_of(h * half + LANES, LANES)
+            acc[1, h] = sum_columns(members[:, pl.ds(start, half - LANES)])
+
+        rest(1 - core)
+        swap_copy(1).start()
+        scatter(0)
+        rest(core)
+        scatter(1)
+        scatter_wait(0)
+        scatter_wait(1)
+
+        block = [gathered[q, 0] for q in range(2)]
         for u in range(1, units):
-            block = block + gathered[u]
-        total = jnp.sum(block[:, half:], axis=1, keepdims=True)
-        centers = block[:, :half] / (total + 1.0)
+            block = [block[q] + gathered[q, u] for q in range(2)]
+        total = jnp.sum(block[0][:, LANES:], axis=1, keepdims=True)
+        centers = jnp.concatenate([block[0][:, :LANES], block[1]], axis=1) / (total + 1.0)
         mine[...] = centers
         norm = 0.5 * jnp.sum(centers * centers, axis=1, keepdims=True)
         hi = norm.astype(jnp.bfloat16).astype(jnp.float32)
@@ -147,22 +169,28 @@
 
         @pl.loop(1, units)
         def _(d):
-            ag_copy(d, lax.rem(unit + d, units), unit).start()
-
-        @pl.loop(1, units)
-        def _(d):
-            ag_copy(d, lax.rem(unit + d, units), lax.rem(unit + units - d, units)).wait()
+            pltpu.make_async_remote_copy(
+                src_ref=packs.at[core, unit], dst_ref=packs.at[core, unit],
+                send_sem=ag_send.at[0], recv_sem=ag_recv.at[0],
+                device_id=device_of(wrap(unit + d), core), device_id_type=MESH,
+            ).start()
+
+        pltpu.make_async_remote_copy(
+            src_ref=packs.at[core, : units - 1], dst_ref=packs.at[core, : units - 1],
+            send_sem=ag_send.at[0], recv_sem=ag_recv.at[0],
+            device_id=sibling, device_id_type=MESH,
+        ).wait()
 
         forward = pltpu.make_async_remote_copy(
             src_ref=packs.at[core], dst_ref=packs.at[core],
-            send_sem=sib_send.at[1], recv_sem=sib_recv.at[1],
+            send_sem=sib_send.at[2], recv_sem=sib_recv.at[2],
             device_id=sibling, device_id_type=MESH,
         )
         forward.start()
         forward.wait_send()
         pltpu.make_async_remote_copy(
             src_ref=packs.at[core], dst_ref=packs.at[1 - core],
-            send_sem=sib_send.at[1], recv_sem=sib_recv.at[1],
+            send_sem=sib_send.at[2], recv_sem=sib_recv.at[2],
             device_id=sibling, device_id_type=MESH,
         ).wait_recv()
 
@@ -177,12 +205,13 @@
             wide_table[l] = jnp.concatenate(whole, axis=1)
         table[...] = wide_table[...].reshape(table.shape).astype(jnp.bfloat16)
 
-    accumulate(seeded)
+    weigh_all(seeded)
+    arrive()
     exchange()
 
     @pl.loop(0, ITERS)
     def _(turn):
-        accumulate(assign)
+        weigh_all(assign)
         exchange()
 
     def fin_copy(d, slot):
@@ -220,29 +249,33 @@
             jax.ShapeDtypeStruct((K, rows), jnp.float32),
             jax.ShapeDtypeStruct((n_help, K, half), jnp.float32),
         ),
-        in_specs=[vmem] * 3,
+        in_specs=[pl.BlockSpec(memory_space=pl.ANY), vmem, vmem],
         out_specs=(vmem, vmem),
         scratch_shapes=[
-            pltpu.VMEM((2, lists * K, packed), jnp.float32),
-            pltpu.VMEM((lists * K, packed), jnp.float32),
-            pltpu.VMEM((units, K, packed), jnp.float32),
-            pltpu.VMEM((units, K, packed), jnp.float32),
+            pltpu.VMEM((rows, width), jnp.bfloat16),
+            pltpu.VMEM((lists * K, rows), jnp.bfloat16),
+            pltpu.VMEM((lists * K, LANES), jnp.float32),
+            pltpu.VMEM((2, 2, lists * K, half - LANES), jnp.float32),
+            pltpu.VMEM((2, lists * K, half - LANES), jnp.float32),
+            pltpu.VMEM((2, units, K, half - LANES), jnp.float32),
+            pltpu.VMEM((2, units, K, half - LANES), jnp.float32),
             pltpu.VMEM((2, units, 2 * K, packed // 2), jnp.bfloat16),
             pltpu.VMEM((lists * K, width), jnp.bfloat16),
             pltpu.VMEM((lists * K, LANES), jnp.float32),
             pltpu.VMEM((K, half), jnp.float32),
             pltpu.VMEM((lists, K, width), jnp.float32),
+            dma((3,)),
+            dma((3,)),
             dma((2,)),
             dma((2,)),
-            dma((units,)),
-            dma((units,)),
-            dma((units,)),
-            dma((units,)),
+            dma((1,)),
+            dma((1,)),
             dma((n_help,)),
             dma((n_help,)),
+            dma,
         ],
         compiler_params=pltpu.CompilerParams(
-            collective_id=0, has_side_effects=True, vmem_limit_bytes=48 * 1024 * 1024
+            collective_id=0, has_side_effects=True, vmem_limit_bytes=60 * 1024 * 1024
         ),
     )(members, owner.reshape(1, rows), seed_label.reshape(1, rows))
     cent = cent.reshape(n_help // 2, 2, K, half).transpose(0, 2, 1, 3)

time: 97.4 us -> 89.2 us (0.916)
  Pallas kernels: 93.7 us -> 85.2 us
    pallas_call x1, Pallas kernels: 93.7 us -> 85.2 us  [local(): pl.pallas_call(functools.partial(kernel, n_list, n_help), out_shape=(jax....]
    unnamed x6 -> x2, local copies, waits for them, and re-layouts: 2.7 us -> 2.99 us
where the time goes in v3:
time: 89.2 us; the launch traced here: 88.9 us
  Pallas kernels  85.2 us (96%)
  local copies, waits for them, and re-layouts  2.99 us (3%)
    pallas_call x1, Pallas kernels, local(): pl.pallas_call(functools.partial(kernel, n_list, n_help), out_shape=(jax....  85.2 us
    unnamed x2, local copies, waits for them, and re-layouts  2.99 us

profile of v3, /device:TPU:0, one launch (start us, length us, event | category | flops | bytes accessed | tf_op | source)
XLA Modules:
  0.0 88.9 jit_solution(6791647293042701246)
XLA Ops:
  0.6 85.2 %shard_map.50 = (f32[8,4096]{1,0:T(8,128)}, f32[4,8,384]{2,1,0:T(8,128)}) custom-call(bf16[4096,768]{1,0:T(8,128)(2,1)} %source.1, s32[1,4096]{1,0:T(1,128)} %bitcast.8, s32[1,4096]{1,0:T(1,128)} %bitcast.9), custom_call_target="tpu_custom_call" | custom-call | tf_op jit(solution)/shard_map/pallas_call | solution.py:246
  85.9 1.6 %copy.7 = f32[8,4096]{1,0:T(8,128)} copy(f32[8,4096]{1,0:T(8,128)} %get-tuple-element.8) | data formatting | bytes 262144
  87.4 1.4 %copy.8 = f32[2,8,768]{2,1,0:T(8,128)} copy(f32[2,8,768]{2,1,0:T(8,128)} %bitcast.7) | data formatting | bytes 98304

commit v4 on v3

--- a/solution.py
+++ b/solution.py
@@ -16,7 +16,7 @@
 
 def kernel(
     n_list, n_help, source, own, seed, out, cent,
-    members, weights, count, acc, theirs, part, gathered, packs, table, power, mine, wide_table,
+    members, weights, count, acc, theirs, part, gathered, packs, table, power, mine, wide_table, logits,
     sib_send, sib_recv, rs_send, rs_recv, ag_send, ag_recv, fin_send, fin_recv, load_sem,
 ):
     rows, width = members.shape
@@ -42,7 +42,7 @@
 
     barrier = pltpu.get_barrier_semaphore()
 
-    @pl.loop(1, units)
+    @pl.loop(1, units, unroll=3)
     def _(d):
         pl.semaphore_signal(
             barrier, inc=1, device_id=device_of(wrap(unit + d), core), device_id_type=MESH
@@ -70,7 +70,7 @@
         swap_copy(q).wait()
         part[q] = (acc[q, core] + theirs[q]).reshape(part.shape[1:])
 
-        @pl.loop(1, units)
+        @pl.loop(1, units, unroll=3)
         def _(d):
             to = wrap(unit + d)
             pltpu.make_async_remote_copy(
@@ -88,17 +88,32 @@
             device_id=sibling, device_id_type=MESH,
         ).wait()
 
-    def assign(t):
+    def half_logit(t, h):
         cols = pl.ds(pl.multiple_of(t * TILE, TILE), TILE)
+        start = pl.multiple_of(h * half, LANES)
         inner = lax.dot_general(
-            table[...], members[cols, :], (((1,), (1,)), ((), ())),
+            table[h], members[cols, pl.ds(start, half)], (((1,), (1,)), ((), ())),
             preferred_element_type=jnp.float32,
         )
         owner = jnp.broadcast_to(own[:, cols], (K, TILE))
         logit = jnp.zeros((K, TILE), jnp.float32)
         for l in range(lists):
             row = slice(l * K, (l + 1) * K)
-            logit = jnp.where(owner == l, inner[row] - power[row, 0:1], logit)
+            logit = jnp.where(owner == l, inner[row] - power[h, row, 0:1], logit)
+        return logit
+
+    def unpack(h):
+        for l in range(lists):
+            got = packs[h, l].astype(jnp.float32)
+            got = jnp.concatenate([got[:K], got[K:]], axis=1)
+            norm = jnp.sum(got[:, half:], axis=1, keepdims=True)
+            power[h, l * K : (l + 1) * K, :] = jnp.broadcast_to(norm, (K, LANES))
+            wide_table[l] = got[:, :half]
+        table[h] = wide_table[...].reshape(table.shape[1:]).astype(jnp.bfloat16)
+
+    def assign(t):
+        cols = pl.ds(pl.multiple_of(t * TILE, TILE), TILE)
+        logit = logits[:, cols] + half_logit(t, 1 - core)
         e = jnp.exp(logit - jnp.max(logit, axis=0, keepdims=True))
         return e / jnp.sum(e, axis=0, keepdims=True)
 
@@ -167,7 +182,7 @@
             [wide[:, :side], wide[:, side:]], axis=0
         ).astype(jnp.bfloat16)
 
-        @pl.loop(1, units)
+        @pl.loop(1, units, unroll=3)
         def _(d):
             pltpu.make_async_remote_copy(
                 src_ref=packs.at[core, unit], dst_ref=packs.at[core, unit],
@@ -187,23 +202,20 @@
             device_id=sibling, device_id_type=MESH,
         )
         forward.start()
+
+        unpack(core)
+
+        @pl.loop(0, rows // TILE)
+        def _(t):
+            logits[:, pl.ds(pl.multiple_of(t * TILE, TILE), TILE)] = half_logit(t, core)
+
         forward.wait_send()
         pltpu.make_async_remote_copy(
             src_ref=packs.at[core], dst_ref=packs.at[1 - core],
             send_sem=sib_send.at[2], recv_sem=sib_recv.at[2],
             device_id=sibling, device_id_type=MESH,
         ).wait_recv()
-
-        for l in range(lists):
-            whole, norms = [], 0.0
-            for h in range(2):
-                got = packs[h, l].astype(jnp.float32)
-                got = jnp.concatenate([got[:K], got[K:]], axis=1)
-                whole.append(got[:, :half])
-                norms = norms + jnp.sum(got[:, half:], axis=1, keepdims=True)
-            power[l * K : (l + 1) * K, :] = jnp.broadcast_to(norms, (K, LANES))
-            wide_table[l] = jnp.concatenate(whole, axis=1)
-        table[...] = wide_table[...].reshape(table.shape).astype(jnp.bfloat16)
+        unpack(1 - core)
 
     weigh_all(seeded)
     arrive()
@@ -260,10 +272,11 @@
             pltpu.VMEM((2, units, K, half - LANES), jnp.float32),
             pltpu.VMEM((2, units, K, half - LANES), jnp.float32),
             pltpu.VMEM((2, units, 2 * K, packed // 2), jnp.bfloat16),
-            pltpu.VMEM((lists * K, width), jnp.bfloat16),
-            pltpu.VMEM((lists * K, LANES), jnp.float32),
+            pltpu.VMEM((2, lists * K, half), jnp.bfloat16),
+            pltpu.VMEM((2, lists * K, LANES), jnp.float32),
             pltpu.VMEM((K, half), jnp.float32),
-            pltpu.VMEM((lists, K, width), jnp.float32),
+            pltpu.VMEM((lists, K, half), jnp.float32),
+            pltpu.VMEM((K, rows), jnp.float32),
             dma((3,)),
             dma((3,)),
             dma((2,)),

time: 89.2 us -> 87.7 us (0.983)
  Pallas kernels: 85.2 us -> 83.8 us
    pallas_call x1, Pallas kernels: 85.2 us -> 83.8 us  [local(): pl.pallas_call(functools.partial(kernel, n_list, n_help), out_shape=(jax....]
where the time goes in v4:
time: 87.7 us; the launch traced here: 87.4 us
  Pallas kernels  83.8 us (96%)
  local copies, waits for them, and re-layouts  2.99 us (3%)
    pallas_call x1, Pallas kernels, local(): pl.pallas_call(functools.partial(kernel, n_list, n_help), out_shape=(jax....  83.8 us
    unnamed x2, local copies, waits for them, and re-layouts  2.99 us

profile of v4, /device:TPU:0, one launch (start us, length us, event | category | flops | bytes accessed | tf_op | source)
XLA Modules:
  0.0 87.4 jit_solution(14871059933208727962)
XLA Ops:
  0.6 83.8 %shard_map.50 = (f32[8,4096]{1,0:T(8,128)}, f32[4,8,384]{2,1,0:T(8,128)}) custom-call(bf16[4096,768]{1,0:T(8,128)(2,1)} %source.1, s32[1,4096]{1,0:T(1,128)} %bitcast.8, s32[1,4096]{1,0:T(1,128)} %bitcast.9), custom_call_target="tpu_custom_call" | custom-call | tf_op jit(solution)/shard_map/pallas_call | solution.py:258
  84.4 1.6 %copy.7 = f32[8,4096]{1,0:T(8,128)} copy(f32[8,4096]{1,0:T(8,128)} %get-tuple-element.8) | data formatting | bytes 262144
  86.0 1.4 %copy.8 = f32[2,8,768]{2,1,0:T(8,128)} copy(f32[2,8,768]{2,1,0:T(8,128)} %bitcast.7) | data formatting | bytes 98304

commit v5 on v4

--- a/solution.py
+++ b/solution.py
@@ -288,7 +288,7 @@
             dma,
         ],
         compiler_params=pltpu.CompilerParams(
-            collective_id=0, has_side_effects=True, vmem_limit_bytes=60 * 1024 * 1024
+            collective_id=0, has_side_effects=True, vmem_limit_bytes=52 * 1024 * 1024
         ),
     )(members, owner.reshape(1, rows), seed_label.reshape(1, rows))
     cent = cent.reshape(n_help // 2, 2, K, half).transpose(0, 2, 1, 3)

time: 87.7 us -> 86 us (0.981)
  Pallas kernels: 83.8 us -> 82.3 us
    pallas_call x1, Pallas kernels: 83.8 us -> 82.3 us  [local(): pl.pallas_call(functools.partial(kernel, n_list, n_help), out_shape=(jax....]
    unnamed x2 -> x6, local copies, waits for them, and re-layouts: 2.99 us -> 2.7 us
where the time goes in v5:
time: 86 us; the launch traced here: 85.7 us
  Pallas kernels  82.3 us (96%)
  local copies, waits for them, and re-layouts  2.7 us (3%)
    pallas_call x1, Pallas kernels, local(): pl.pallas_call(functools.partial(kernel, n_list, n_help), out_shape=(jax....  82.3 us
    unnamed x6, local copies, waits for them, and re-layouts  2.7 us

profile of v5, /device:TPU:0, one launch (start us, length us, event | category | flops | bytes accessed | tf_op | source)
XLA Modules:
  0.0 85.7 jit_solution(11036449225149060140)
XLA Ops:
  0.6 0.0 copy-start
  0.6 0.7 copy-done
  1.3 0.0 copy-start.1
  1.4 0.7 copy-done.1
  2.1 82.3 %shard_map.50 = (f32[8,4096]{1,0:T(8,128)S(1)}, f32[4,8,384]{2,1,0:T(8,128)S(1)}) custom-call(bf16[4096,768]{1,0:T(8,128)(2,1)} %source.1, s32[1,4096]{1,0:T(1,128)S(1)} %bitcast.8, s32[1,4096]{1,0:T(1,128)S(1)} %bitcast.9), custom_call_target="tpu_custom_call" | custom-call | tf_op jit(solution)/shard_map/pallas_call | solution.py:258
  84.4 0.7 copy.7
  85.1 0.6 copy.8
Async XLA Ops:
  0.6 0.7 copy-start
  1.3 0.7 copy-start.1
